TPU v7x, 512 devices: a whole 4x8x8 slice. The times are simulated.
512 devices in a mesh: clip: 32 (over x, z), seq: 16 (over y, core).
Axes of the slice: x: 4, y: 8, z: 8, core: 2. Of those that a mesh axis runs over, the one named last changes fastest.
Arguments:
- queries: bfloat16 [32, 32, 64, 2560], P('clip', 'seq'), may hold values from -6 to 6
- key_rows: bfloat16 [32, 32, 64, 2560], P('clip', 'seq'), may hold values from -6 to 6
- values: bfloat16 [32, 32, 64, 2560], P('clip', 'seq'), may hold values from -6 to 6
- cotangent: bfloat16 [32, 32, 64, 2560], P('clip', 'seq'), may hold values from -6 to 6
- lengths: int32 [32], P('clip'), may hold values from 8 to 32, as said below
- episode_cuts: int32 [32, 2], P('clip'), may hold values from 1 to 31
- gain_q: float32 [2560], P('clip'), may hold values from 0.5 to 1.5
- gain_k: float32 [2560], P('clip'), may hold values from 0.5 to 1.5
Outputs:
- grad_queries: bfloat16 [32, 32, 64, 2560], P('clip', 'seq')
- grad_keys: bfloat16 [32, 32, 64, 2560], P('clip', 'seq')
- grad_values: bfloat16 [32, 32, 64, 2560], P('clip', 'seq')
- grad_gain_q: float32 [2560], P('clip')
- grad_gain_k: float32 [2560], P('clip')
Inputs may be any that keep to these rules, and one draw needn't show every extreme that they name: `lengths`: frames at or past a clip's length are padding. `episode_cuts`: A cut at or past the clip's length has no effect; the two cuts of a clip may coincide.
All inputs are finite; a program needn't handle non-finite values.
Results may differ from a plain program's by a relative error of at most 0.007.
Values may be sent and summed in bfloat16 or wider, within the bound.
A program may use at most 128 MiB of HBM per device.

v0:
```python
import math

import jax
import jax.numpy as jnp
from jax import lax
from jax.sharding import PartitionSpec as P

HEADS = 20


EPS = 1e-06


def split_heads(array, head_count):
    return array.reshape(array.shape[:-1] + (head_count, array.shape[-1] // head_count))


def normalize(raw_rows, gain_rows, head_count):
    values_f = split_heads(raw_rows.astype(jnp.float32), head_count)
    inv_rms = lax.rsqrt(jnp.mean(values_f * values_f, axis=-1, keepdims=True) + EPS)
    normed = (values_f * inv_rms * split_heads(gain_rows, head_count)).astype(jnp.bfloat16)
    return (values_f, inv_rms, normed.reshape(raw_rows.shape))


def restore(values_f, inv_rms, gain_rows, grad_normed, head_count):
    grad_heads = split_heads(grad_normed, head_count)
    scaled = split_heads(gain_rows, head_count) * grad_heads
    grad_raw = inv_rms * scaled - values_f * inv_rms**3 * jnp.mean(
        values_f * scaled, axis=-1, keepdims=True
    )
    gain_part = jnp.sum(values_f * inv_rms * grad_heads, axis=(0, 1, 2))
    return (grad_raw.reshape(grad_normed.shape).astype(jnp.bfloat16), gain_part.reshape(-1))


def attend(q_normed, k_normed, value_rows, grad_rows, lengths, episode_cuts, head_count):
    clip_count, frame_count, col_count, width = q_normed.shape
    head_dim = width // head_count
    split_shape = (clip_count, frame_count, col_count, head_count, head_dim)
    q_heads = q_normed.reshape(split_shape)
    k_heads = k_normed.reshape(split_shape)
    v_heads = value_rows.reshape(split_shape)
    g_heads = grad_rows.reshape(split_shape)
    frame_ids = jnp.arange(frame_count, dtype=jnp.int32)
    episode = jnp.sum(
        (episode_cuts[:, None, :] <= frame_ids[None, :, None]).astype(jnp.int32), axis=-1
    )
    live_frames = frame_ids[None, :] < lengths[:, None]
    visible = (
        (frame_ids[None, None, :] <= frame_ids[None, :, None])
        & (episode[:, None, :] == episode[:, :, None])
        & live_frames[:, :, None]
    )
    score_scale = 1.0 / math.sqrt(head_dim)
    scores = (
        jnp.einsum("btchd,bschd->bchts", q_heads, k_heads, preferred_element_type=jnp.float32)
        * score_scale
    )
    exps = jnp.where(visible[:, None, None], jnp.exp(scores), 0.0)
    denominator = (
        jnp.sum(exps, axis=-1, keepdims=True)
        + (1.0 - live_frames.astype(jnp.float32))[:, None, None, :, None]
    )
    softmax = exps / denominator
    soft_round = softmax.astype(jnp.bfloat16)
    attended = jnp.einsum(
        "bchts,bschd->btchd", soft_round, v_heads, preferred_element_type=jnp.float32
    )
    row_delta = jnp.sum(g_heads.astype(jnp.float32) * attended, axis=-1)
    dprob = jnp.einsum("btchd,bschd->bchts", g_heads, v_heads, preferred_element_type=jnp.float32)
    dscore = softmax * (dprob - jnp.transpose(row_delta, (0, 2, 3, 1))[..., None])
    ds_round = dscore.astype(jnp.bfloat16)
    dq_normed = (
        jnp.einsum("bchts,bschd->btchd", ds_round, k_heads, preferred_element_type=jnp.float32)
        * score_scale
    )
    dk_normed = (
        jnp.einsum("bchts,btchd->bschd", ds_round, q_heads, preferred_element_type=jnp.float32)
        * score_scale
    )
    dv_rows = jnp.einsum(
        "bchts,btchd->bschd", soft_round, g_heads, preferred_element_type=jnp.float32
    ).astype(jnp.bfloat16)
    full_shape = q_normed.shape
    return (
        dq_normed.reshape(full_shape),
        dk_normed.reshape(full_shape),
        dv_rows.reshape(full_shape),
    )


def attend_clips(q_normed, k_normed, value_rows, grad_rows, lengths, episode_cuts, head_count):
    return attend(q_normed, k_normed, value_rows, grad_rows, lengths, episode_cuts, head_count)


def body(queries, key_rows, values, cotangent, lengths, episode_cuts, gain_q, gain_k):
    head_count = HEADS
    full_q, full_k = (
        lax.all_gather(gain_q, "clip", axis=0, tiled=True),
        lax.all_gather(gain_k, "clip", axis=0, tiled=True),
    )
    col_first, col_second, col_values, col_grads = (
        lax.all_to_all(queries, "seq", split_axis=2, concat_axis=1, tiled=True),
        lax.all_to_all(key_rows, "seq", split_axis=2, concat_axis=1, tiled=True),
        lax.all_to_all(values, "seq", split_axis=2, concat_axis=1, tiled=True),
        lax.all_to_all(cotangent, "seq", split_axis=2, concat_axis=1, tiled=True),
    )
    q_float, q_rms, q_normed = normalize(col_first, full_q, head_count)
    k_float, k_rms, k_normed = normalize(col_second, full_k, head_count)
    dq_normed, dk_normed, dv_rows = attend_clips(
        q_normed, k_normed, col_values, col_grads, lengths, episode_cuts, head_count
    )
    dq_cols, part_q = restore(q_float, q_rms, full_q, dq_normed, head_count)
    dk_cols, part_k = restore(k_float, k_rms, full_k, dk_normed, head_count)
    dq_rows, dk_rows, dv_out = (
        lax.all_to_all(dq_cols, "seq", split_axis=1, concat_axis=2, tiled=True),
        lax.all_to_all(dk_cols, "seq", split_axis=1, concat_axis=2, tiled=True),
        lax.all_to_all(dv_rows, "seq", split_axis=1, concat_axis=2, tiled=True),
    )
    seq_q, seq_k = lax.psum((part_q, part_k), "seq")
    grad_gq, grad_gk = (
        lax.psum_scatter(seq_q, "clip", scatter_dimension=0, tiled=True),
        lax.psum_scatter(seq_k, "clip", scatter_dimension=0, tiled=True),
    )
    return (dq_rows, dk_rows, dv_out, grad_gq, grad_gk)


def solution(mesh):
    return jax.shard_map(
        body,
        mesh=mesh,
        in_specs=(
            P("clip", "seq", None, None),
            P("clip", "seq", None, None),
            P("clip", "seq", None, None),
            P("clip", "seq", None, None),
            P("clip"),
            P("clip", None),
            P("clip"),
            P("clip"),
        ),
        out_specs=(
            P("clip", "seq", None, None),
            P("clip", "seq", None, None),
            P("clip", "seq", None, None),
            P("clip"),
            P("clip"),
        ),
        check_vma=False,
    )
```

profile of v0, /device:TPU:1, one launch (start us, length us, event | category | flops | bytes accessed | tf_op | source)
XLA Modules:
  0.0 473.7 jit_solution(4282341521147578896)
XLA Ops:
  0.6 2.7 copy.222
  3.3 10.3 %all-to-all-start.1 = ((bf16[1,2,64,2560]{3,1,0,2:T(2,128)(2,1)}), bf16[1,2,64,2560]{3,1,0,2:T(2,128)(2,1)S(1)}, u32[]{:S(2)}, u32[]{:S(2)}) async-start(bf16[1,2,64,2560]{3,1,0,2:T(2,128)(2,1)} %copy.222), calls=%async_computation.1 | async-start | bytes 1310720 | tf_op jit(solution)/shard_map/all_to_all | solution.py:103
  13.6 1.5 copy.218
  15.1 18.5 %all-to-all-done.1 = bf16[1,2,64,2560]{3,1,0,2:T(2,128)(2,1)S(1)} async-done(((bf16[1,2,64,2560]{3,1,0,2:T(2,128)(2,1)}), bf16[1,2,64,2560]{3,1,0,2:T(2,128)(2,1)S(1)}, u32[]{:S(2)}, u32[]{:S(2)}) %all-to-all-start.1) | async-done | bytes 655392 | tf_op jit(solution)/shard_map/all_to_all | solution.py:103
  33.6 3.5 all-to-all-start
  37.1 1.5 copy.229
  38.7 18.0 %all-to-all-done = bf16[1,2,64,2560]{3,1,0,2:T(2,128)(2,1)S(1)} async-done(((bf16[1,2,64,2560]{3,1,0,2:T(2,128)(2,1)}), bf16[1,2,64,2560]{3,1,0,2:T(2,128)(2,1)S(1)}, u32[]{:S(2)}, u32[]{:S(2)}) %all-to-all-start) | async-done | bytes 655392 | tf_op jit(solution)/shard_map/all_to_all | solution.py:102
  56.7 4.2 all-to-all-start.2
  61.5 1.5 copy.231
  64.8 120.2 %all-reduce.5 = (f32[2560]{0:T(1024)S(1)}, f32[2560]{0:T(1024)S(1)}) all-reduce(f32[2560]{0:T(1024)S(1)} %dynamic-update-slice, f32[2560]{0:T(1024)S(1)} %dynamic-update-slice.1), channel_id=1, replica_groups=mesh['clip'=32,'seq'=16] {'clip'}, use_global_device_ids=true, to_apply=%add | all-reduce | flops 5120 | bytes 40960
  186.7 33.0 %all-to-all-start.3 = ((bf16[1,2,64,2560]{3,1,0,2:T(2,128)(2,1)}), bf16[1,2,64,2560]{3,1,0,2:T(2,128)(2,1)}, u32[]{:S(2)}, u32[]{:S(2)}) async-start(bf16[1,2,64,2560]{3,1,0,2:T(2,128)(2,1)} %copy.231), calls=%async_computation.3 | async-start | bytes 1310720 | tf_op jit(solution)/shard_map/all_to_all | solution.py:104
  219.7 1.7 reshape.454
  221.4 2.4 copy.319
  223.8 1.8 reshape.453
  225.6 2.7 reshape.456
  229.3 2.8 copy_bitcast_fusion.3
  232.1 2.7 reshape.457
  234.8 5.0 %all-to-all-done.3 = bf16[1,2,64,2560]{3,1,0,2:T(2,128)(2,1)} async-done(((bf16[1,2,64,2560]{3,1,0,2:T(2,128)(2,1)}), bf16[1,2,64,2560]{3,1,0,2:T(2,128)(2,1)}, u32[]{:S(2)}, u32[]{:S(2)}) %all-to-all-start.3) | async-done | bytes 655392 | tf_op jit(solution)/shard_map/all_to_all | solution.py:104
  239.8 2.2 copy.320
  242.0 2.3 reshape.449
  244.3 2.3 reshape.448
  246.6 2.4 multiply_convert_fusion
  252.9 2.4 fusion.5
  258.1 3.7 all-to-all-start.5
  261.8 2.8 fusion.6
  267.4 13.7 %all-to-all-done.5 = bf16[1,32,4,2560]{3,2,0,1:T(4,128)(2,1)S(1)} async-done(((bf16[1,32,4,2560]{3,2,0,1:T(4,128)(2,1)}), bf16[1,32,4,2560]{3,2,0,1:T(4,128)(2,1)S(1)}, u32[]{:S(2)}, u32[]{:S(2)}) %all-to-all-start.5) | async-done | bytes 655392 | tf_op jit(solution)/shard_map/all_to_all | solution.py:116
  281.1 3.5 all-to-all-start.4
  284.6 1.7 fusion.14
  287.7 16.4 %all-to-all-done.4 = bf16[1,32,4,2560]{3,2,0,1:T(4,128)(2,1)S(1)} async-done(((bf16[1,32,4,2560]{3,2,0,1:T(4,128)(2,1)}), bf16[1,32,4,2560]{3,2,0,1:T(4,128)(2,1)S(1)}, u32[]{:S(2)}, u32[]{:S(2)}) %all-to-all-start.4) | async-done | bytes 655392 | tf_op jit(solution)/shard_map/all_to_all | solution.py:115
  304.1 3.5 all-to-all-start.6
  308.3 110.6 %all-reduce.4 = (f32[2560]{0:T(1024)S(1)}, f32[2560]{0:T(1024)S(1)}) all-reduce(f32[2560]{0:T(1024)S(1)} %bitcast.111, f32[2560]{0:T(1024)S(1)} %bitcast.112), channel_id=2, replica_groups=mesh['clip'=32,'seq'=16] {'clip'}, use_global_device_ids=true, to_apply=%region_9.10.clone | all-reduce | flops 5120 | bytes 40960
  419.1 50.4 %all-reduce.6 = (f32[80]{0:T(128)}, f32[80]{0:T(128)}) all-reduce(f32[80]{0:T(128)S(1)} %dynamic-slice.3, f32[80]{0:T(128)S(1)} %dynamic-slice.5), channel_id=1, replica_groups=mesh['clip'=32,'seq'=16] {'seq'}, use_global_device_ids=true, to_apply=%region_8.9 | all-reduce | flops 160 | bytes 1280 | tf_op jit(solution)/shard_map/psum | solution.py:119
  (80 shorter events, 18.7 us)
Async XLA Ops:
  0.6 12.9 %copy-start.7 = (bf16[1,2,64,2560]{3,2,1,0:T(8,128)(2,1)S(1)}, bf16[1,2,64,2560]{3,2,1,0:T(8,128)(2,1)}, u32[]{:S(2)}) copy-start(bf16[1,2,64,2560]{3,2,1,0:T(8,128)(2,1)} %param.8) | copy-start | bytes 1966084
  3.3 30.3 %all-to-all-start.1 = ((bf16[1,2,64,2560]{3,1,0,2:T(2,128)(2,1)}), bf16[1,2,64,2560]{3,1,0,2:T(2,128)(2,1)S(1)}, u32[]{:S(2)}, u32[]{:S(2)}) async-start(bf16[1,2,64,2560]{3,1,0,2:T(2,128)(2,1)} %copy.222), calls=%async_computation.1 | async-start | bytes 1310720 | tf_op jit(solution)/shard_map/all_to_all | solution.py:103
  13.6 23.5 %copy-start.8 = (bf16[1,2,64,2560]{3,2,1,0:T(8,128)(2,1)S(1)}, bf16[1,2,64,2560]{3,2,1,0:T(8,128)(2,1)}, u32[]{:S(2)}) copy-start(bf16[1,2,64,2560]{3,2,1,0:T(8,128)(2,1)} %param.11) | copy-start | bytes 1966084
  33.6 23.1 %all-to-all-start = ((bf16[1,2,64,2560]{3,1,0,2:T(2,128)(2,1)}), bf16[1,2,64,2560]{3,1,0,2:T(2,128)(2,1)S(1)}, u32[]{:S(2)}, u32[]{:S(2)}) async-start(bf16[1,2,64,2560]{3,1,0,2:T(2,128)(2,1)} %copy.218), calls=%async_computation | async-start | bytes 1310720 | tf_op jit(solution)/shard_map/all_to_all | solution.py:102
  37.1 24.4 %copy-start.9 = (bf16[1,2,64,2560]{3,2,1,0:T(8,128)(2,1)S(1)}, bf16[1,2,64,2560]{3,2,1,0:T(8,128)(2,1)}, u32[]{:S(2)}) copy-start(bf16[1,2,64,2560]{3,2,1,0:T(8,128)(2,1)} %param.10) | copy-start | bytes 1966084
  38.6 24.4 %copy-start.11 = (u32[512]{0:T(512)S(1)}, u32[512]{0:T(512)}, u32[]{:S(2)}) copy-start(u32[512]{0:T(512)} %constant.27) | copy-start | bytes 6148
  38.6 25.6 %copy-start.12 = (f32[80]{0:T(128)S(1)}, f32[80]{0:T(128)}, u32[]{:S(2)}) copy-start(f32[80]{0:T(128)} %param.15) | copy-start | bytes 964
  38.6 25.9 %copy-start.13 = (f32[80]{0:T(128)S(1)}, f32[80]{0:T(128)}, u32[]{:S(2)}) copy-start(f32[80]{0:T(128)} %param.14) | copy-start | bytes 964
  38.6 146.4 %copy-start.14 = (s32[1,2]{1,0:T(1,128)S(1)}, s32[1,2]{1,0:T(1,128)}, u32[]{:S(2)}) copy-start(s32[1,2]{1,0:T(1,128)} %param.13) | copy-start | bytes 28
  56.7 6.4 %copy-start.2 = (bf16[1,2,64,2560]{3,1,0,2:T(2,128)(2,1)}, bf16[1,2,64,2560]{3,1,0,2:T(2,128)(2,1)S(1)}, u32[]{:S(2)}) copy-start(bf16[1,2,64,2560]{3,1,0,2:T(2,128)(2,1)S(1)} %all-to-all-done) | copy-start | bytes 1966084
  56.7 130.0 %all-to-all-start.2 = ((bf16[1,2,64,2560]{3,1,0,2:T(2,128)(2,1)}), bf16[1,2,64,2560]{3,1,0,2:T(2,128)(2,1)}, u32[]{:S(2)}, u32[]{:S(2)}) async-start(bf16[1,2,64,2560]{3,1,0,2:T(2,128)(2,1)} %copy.229), calls=%async_computation.2 | async-start | bytes 1310720 | tf_op jit(solution)/shard_map/all_to_all | solution.py:105
  186.7 53.1 %all-to-all-start.3 = ((bf16[1,2,64,2560]{3,1,0,2:T(2,128)(2,1)}), bf16[1,2,64,2560]{3,1,0,2:T(2,128)(2,1)}, u32[]{:S(2)}, u32[]{:S(2)}) async-start(bf16[1,2,64,2560]{3,1,0,2:T(2,128)(2,1)} %copy.231), calls=%async_computation.3 | async-start | bytes 1310720 | tf_op jit(solution)/shard_map/all_to_all | solution.py:104
  249.0 0.9 copy-start
  249.0 1.7 copy-start.3
  249.0 2.1 copy-start.6
  249.9 2.4 copy-start.15
  251.0 1.2 copy-start.4
  252.9 2.5 copy-start.10
  256.9 4.9 %copy-start.1 = (bf16[32,4,20,128]{3,2,1,0:T(8,128)(2,1)S(1)}, bf16[32,4,20,128]{3,2,1,0:T(8,128)(2,1)}, u32[]{:S(2)}) copy-start(bf16[32,4,20,128]{3,2,1,0:T(8,128)(2,1)} %copy-done) | copy-start | bytes 1966084
  258.1 23.0 %all-to-all-start.5 = ((bf16[1,32,4,2560]{3,2,0,1:T(4,128)(2,1)}), bf16[1,32,4,2560]{3,2,0,1:T(4,128)(2,1)S(1)}, u32[]{:S(2)}, u32[]{:S(2)}) async-start(bf16[1,32,4,2560]{3,2,0,1:T(4,128)(2,1)} %reshape.473), calls=%async_computation.5 | async-start | bytes 1310720 | tf_op jit(solution)/shard_map/all_to_all | solution.py:116
  266.2 18.4 %copy-start.5 = (bf16[32,4,20,128]{3,2,1,0:T(8,128)(2,1)S(1)}, bf16[32,4,20,128]{3,2,1,0:T(8,128)(2,1)}, u32[]{:S(2)}) copy-start(bf16[32,4,20,128]{3,2,1,0:T(8,128)(2,1)} %reshape.448) | copy-start | bytes 1966084
  281.1 23.0 %all-to-all-start.4 = ((bf16[1,32,4,2560]{3,2,0,1:T(4,128)(2,1)}), bf16[1,32,4,2560]{3,2,0,1:T(4,128)(2,1)S(1)}, u32[]{:S(2)}, u32[]{:S(2)}) async-start(bf16[1,32,4,2560]{3,2,0,1:T(4,128)(2,1)} %reshape.472), calls=%async_computation.4 | async-start | bytes 1310720 | tf_op jit(solution)/shard_map/all_to_all | solution.py:115
  304.1 168.1 %all-to-all-start.6 = ((bf16[1,32,4,2560]{3,2,0,1:T(4,128)(2,1)}), bf16[1,32,4,2560]{3,2,0,1:T(4,128)(2,1)S(1)}, u32[]{:S(2)}, u32[]{:S(2)}) async-start(bf16[1,32,4,2560]{3,2,0,1:T(4,128)(2,1)} %reshape.474), calls=%async_computation.6 | async-start | bytes 1310720 | tf_op jit(solution)/shard_map/all_to_all | solution.py:117
where the time goes:
time: 475 us; the launch traced here: 474 us
  blocking collectives  281 us (59%)
  waiting for transfers between devices  71.7 us (15%)
  starting transfers between devices  61.6 us (13%)
  local copies, waits for them, and re-layouts  37.6 us (8%)
  matrix products  9.48 us (2%)
  other arithmetic  9.11 us (2%)
    unnamed x2, blocking collectives  231 us
    psum x1, blocking collectives, body(): seq_q, seq_k = lax.psum((part_q, part_k), 'seq')  50.4 us
    all_to_all x1, starting transfers between devices, body(): lax.all_to_all(values, 'seq', split_axis=2, concat_axis=1, tiled=True)  33 us
    all_to_all x1, waiting for transfers between devices, body(): lax.all_to_all(key_rows, 'seq', split_axis=2, concat_axis=1, tiled=True)  18.5 us
    all_to_all x1, waiting for transfers between devices, body(): lax.all_to_all(queries, 'seq', split_axis=2, concat_axis=1, tiled=True)  18 us
    all_to_all x1, waiting for transfers between devices, body(): lax.all_to_all(dq_cols, 'seq', split_axis=1, concat_axis=2, tiled=True)  16.4 us
    all_to_all x1, waiting for transfers between devices, body(): lax.all_to_all(dk_cols, 'seq', split_axis=1, concat_axis=2, tiled=True)  13.7 us
    unnamed x46, local copies, waits for them, and re-layouts  12.6 us
  transfers between devices with their start and end apart: 7, of which 5 were waited for; matrix products, arithmetic and copies ran while one was open for 7% of the time, Pallas kernels for 0%

commit v1 on v0

v1 whole, which is shorter than its diff:
```python
import math

import jax
import jax.numpy as jnp
from jax import lax
from jax.experimental import pallas as pl
from jax.experimental.pallas import tpu as pltpu
from jax.sharding import PartitionSpec as P

HEADS = 20
HD = 128
EPS = 1e-06
FRAMES = 32
XS = 4
ZS = 8
SEQ = 16
OWN = FRAMES // SEQ
TILE = 16
PATCHES = 64
TILES = PATCHES // TILE
GROUPS = SEQ // TILES
GH = HEADS // GROUPS
ROWS = FRAMES * TILE
BLK = 128
NBLK = ROWS // BLK
BF = BLK // TILE
SLICE = HEADS * HD // (XS * ZS)
MESH = pl.DeviceIdType.MESH
F32 = jnp.float32
BF16 = jnp.bfloat16


def lanes(array, start):
    row, off = divmod(start, HD)
    first = array(row)
    if off == 0:
        return first
    low = pltpu.roll(first, HD - off, 1)
    if row + 1 >= GH:
        return low
    high = pltpu.roll(array(row + 1), HD - off, 1)
    lane = lax.broadcasted_iota(jnp.int32, first.shape, 1)
    return jnp.where(lane < HD - off, low, high)


def kernel(
    len_ref, cut_ref, gq_ref, gk_ref, q_hbm, k_hbm, v_hbm, g_hbm,
    o_hbm, gain_out,
    stage, recv, obuf, qh_s, kh_s, soft_s, ds_s, bias, gains, parts,
    gsend, grecv, psend, precv, fsend, frecv,
    stage_sem, send_sem, recv_sem, osend_sem, orecv_sem,
    gsend_sem, grecv_sem, psend_sem, precv_sem, fsend_sem, frecv_sem,
):
    clip = lax.axis_index("clip")
    me = lax.axis_index("seq")
    x, z = lax.div(clip, ZS), lax.rem(clip, ZS)
    g, j = lax.div(me, TILES), lax.rem(me, TILES)
    far_seq = x * TILES + j
    same = (g == x).astype(jnp.int32)

    def far(zz):
        return (g * ZS + zz, far_seq)

    def is_me(zz):
        return jnp.logical_and(g == x, z == zz)

    for n, ref in enumerate((q_hbm, k_hbm, v_hbm, g_hbm)):
        pltpu.make_async_copy(ref, stage.at[n], stage_sem).start()

    barrier = pltpu.get_barrier_semaphore()
    for d in range(1, SEQ):
        pl.semaphore_signal(
            barrier, inc=1, device_id=(clip, lax.rem(me + d, SEQ)), device_id_type=MESH
        )
    for zz in range(ZS):

        @pl.when(jnp.logical_not(is_me(zz)))
        def _():
            pl.semaphore_signal(barrier, inc=1, device_id=far(zz), device_id_type=MESH)

    gsend[...] = jnp.zeros_like(gsend)
    gsend[0:1, 0:SLICE] = gq_ref[...]
    gsend[1:2, 0:SLICE] = gk_ref[...]

    def exchange(src, dst, s_sem, r_sem):
        for zz in range(ZS):

            @pl.when(is_me(zz))
            def _():
                pltpu.make_async_copy(src(zz), dst.at[z], r_sem).start()

            @pl.when(jnp.logical_not(is_me(zz)))
            def _():
                pltpu.make_async_remote_copy(
                    src_ref=src(zz), dst_ref=dst.at[z], send_sem=s_sem, recv_sem=r_sem,
                    device_id=far(zz), device_id_type=MESH,
                ).start()

    def exchange_sent(dst, s_sem):
        @pl.when(same == 1)
        def _():
            part = dst.at[pl.ds(0, ZS - 1)]
            pltpu.make_async_copy(part, part, s_sem).wait()

        @pl.when(same == 0)
        def _():
            pltpu.make_async_copy(dst, dst, s_sem).wait()

    pltpu.make_async_copy(stage, stage, stage_sem).wait()
    pl.semaphore_wait(barrier, SEQ - 1 + ZS - same)

    exchange(lambda zz: gsend, grecv, gsend_sem, grecv_sem)

    def send_in(h, _):
        def source(to):
            to_g, to_j = lax.div(to, TILES), lax.rem(to, TILES)
            return stage.at[
                :, :, pl.ds(pl.multiple_of(to_j * TILE, TILE), TILE),
                pl.ds(pl.multiple_of((to_g * GH + h) * HD, HD), HD),
            ]

        place = recv.at[h, :, pl.ds(me * OWN, OWN)]
        for d in range(1, SEQ):
            to = lax.rem(me + d, SEQ)
            pltpu.make_async_remote_copy(
                src_ref=source(to), dst_ref=place, send_sem=send_sem, recv_sem=recv_sem.at[h],
                device_id=(clip, to), device_id_type=MESH,
            ).start()
        pltpu.make_async_copy(source(me), place, recv_sem.at[h]).start()
        return 0

    lax.fori_loop(0, GH, send_in, 0)

    length = len_ref[0]
    cut_a, cut_b = cut_ref[0, 0], cut_ref[0, 1]
    for tb in range(NBLK):
        rows = BLK * (tb + 1)
        s_at = lax.broadcasted_iota(jnp.int32, (rows, BLK), 0)
        t_at = lax.broadcasted_iota(jnp.int32, (rows, BLK), 1) + tb * BLK
        s_f, t_f = s_at // TILE, t_at // TILE
        s_e = (cut_a <= s_f).astype(jnp.int32) + (cut_b <= s_f).astype(jnp.int32)
        t_e = (cut_a <= t_f).astype(jnp.int32) + (cut_b <= t_f).astype(jnp.int32)
        ok = (s_f <= t_f) & (s_e == t_e) & (t_f < length) & (s_at % TILE == t_at % TILE)
        bias[0:rows, tb * BLK : (tb + 1) * BLK] = jnp.where(ok, 0.0, -1e30)

    pltpu.make_async_copy(grecv, grecv, grecv_sem).wait()
    gains[...] = jnp.zeros_like(gains)
    for zz in range(ZS):
        row, off = divmod(zz * SLICE, HD)
        for n in range(2):
            piece = grecv[zz, n : n + 1, :]
            moved = pltpu.roll(piece, off, 1) if off else piece
            lane = lax.broadcasted_iota(jnp.int32, (1, HD), 1)
            gains[n, row : row + 1, :] += jnp.where(lane >= off, moved, 0.0)
            if off + SLICE > HD:
                gains[n, row + 1 : row + 2, :] += jnp.where(lane < off + SLICE - HD, moved, 0.0)

    scale = 1.0 / math.sqrt(HD)
    along = (((1,), (1,)), ((), ()))
    down = (((0,), (0,)), ((), ()))
    plain = (((1,), (0,)), ((), ()))

    def dot(a, b, dims):
        return lax.dot_general(a, b, dims, preferred_element_type=F32)

    def mean(a):
        return jnp.sum(a, axis=-1, keepdims=True) * (1.0 / HD)

    def flat(ref, lo, hi):
        return ref[lo // TILE : hi // TILE].reshape(hi - lo, HD)

    def restore(raw, inv, gain, grad, n, h, lo):
        scaled = gain * grad
        normed = raw * inv
        out = inv * (scaled - normed * mean(normed * scaled))
        obuf[h, n, lo // TILE : (lo + BLK) // TILE] = out.astype(BF16).reshape(BF, TILE, HD)
        return jnp.sum(normed * grad, axis=0, keepdims=True)

    def head(h, _):
        pltpu.make_async_copy(recv.at[h], recv.at[h], recv_sem.at[h]).wait()
        q_r, k_r, v_r, g_r = (recv.at[h, n] for n in range(4))
        gain_q = gains[0, pl.ds(h, 1), :]
        gain_k = gains[1, pl.ds(h, 1), :]
        inv_q, inv_k = [], []
        for b in range(NBLK):
            lo, hi = b * BLK, (b + 1) * BLK
            for src, invs, gain, dst in ((q_r, inv_q, gain_q, qh_s), (k_r, inv_k, gain_k, kh_s)):
                raw = flat(src, lo, hi).astype(F32)
                inv = lax.rsqrt(mean(raw * raw) + EPS)
                invs.append(inv)
                dst[lo:hi] = (raw * inv * gain).astype(BF16)

        part_q = jnp.zeros((1, HD), F32)
        part_k = jnp.zeros((1, HD), F32)
        for b in range(NBLK):
            lo, hi = b * BLK, (b + 1) * BLK
            scores = dot(kh_s[0:hi], qh_s[lo:hi], along)
            exps = jnp.exp(scores * scale + bias[0:hi, lo:hi])
            frame = (lax.broadcasted_iota(jnp.int32, (1, BLK), 1) + lo) // TILE
            dead = (frame >= length).astype(F32)
            total = jnp.sum(exps, axis=0, keepdims=True) + dead
            soft = exps * (1.0 / total)
            soft_b = soft.astype(BF16)
            dprob = dot(flat(v_r, 0, hi), flat(g_r, lo, hi), along)
            delta = jnp.sum(soft_b.astype(F32) * dprob, axis=0, keepdims=True)
            ds_b = (soft * (dprob - delta)).astype(BF16)
            soft_s[0:hi, lo:hi] = soft_b
            ds_s[0:hi, lo:hi] = ds_b
            dq = dot(ds_b, kh_s[0:hi], down) * scale
            raw = flat(q_r, lo, hi).astype(F32)
            part_q += restore(raw, inv_q[b], gain_q, dq, 0, h, lo)
        for b in range(NBLK):
            lo, hi = b * BLK, (b + 1) * BLK
            dk = dot(ds_s[lo:hi, lo:ROWS], qh_s[lo:ROWS], plain) * scale
            raw = flat(k_r, lo, hi).astype(F32)
            part_k += restore(raw, inv_k[b], gain_k, dk, 1, h, lo)
            dv = dot(soft_s[lo:hi, lo:ROWS], flat(g_r, lo, ROWS), plain)
            obuf[h, 2, lo // TILE : hi // TILE] = dv.astype(BF16).reshape(BF, TILE, HD)
        parts[0, pl.ds(h, 1), :] = part_q
        parts[1, pl.ds(h, 1), :] = part_k

        place = o_hbm.at[
            :, :, pl.ds(pl.multiple_of(j * TILE, TILE), TILE),
            pl.ds(pl.multiple_of((g * GH + h) * HD, HD), HD),
        ]
        for d in range(1, SEQ):
            to = lax.rem(me + d, SEQ)
            pltpu.make_async_remote_copy(
                src_ref=obuf.at[h, :, pl.ds(to * OWN, OWN)], dst_ref=place,
                send_sem=osend_sem, recv_sem=orecv_sem,
                device_id=(clip, to), device_id_type=MESH,
            ).start()
        pltpu.make_async_copy(obuf.at[h, :, pl.ds(me * OWN, OWN)], place, orecv_sem).start()
        return 0

    lax.fori_loop(0, GH, head, 0)

    for zz in range(ZS):
        for n in range(2):
            psend[zz, n : n + 1, :] = lanes(lambda r: parts[n, r : r + 1, :], zz * SLICE)
    exchange(lambda zz: psend.at[zz], precv, psend_sem, precv_sem)
    pltpu.make_async_copy(precv, precv, precv_sem).wait()
    fsend[...] = jnp.sum(precv[...], axis=0)
    for d in range(1, SEQ):
        pltpu.make_async_remote_copy(
            src_ref=fsend, dst_ref=frecv.at[me], send_sem=fsend_sem, recv_sem=frecv_sem,
            device_id=(clip, lax.rem(me + d, SEQ)), device_id_type=MESH,
        ).start()
    pltpu.make_async_copy(fsend, frecv.at[me], frecv_sem).start()
    pltpu.make_async_copy(frecv, frecv, frecv_sem).wait()
    gain_out[...] = jnp.sum(frecv[...], axis=0)

    pltpu.make_async_copy(o_hbm, o_hbm, orecv_sem).wait()
    exchange_sent(grecv, gsend_sem)
    exchange_sent(precv, psend_sem)
    sent = frecv.at[pl.ds(0, SEQ - 1)]
    pltpu.make_async_copy(sent, sent, fsend_sem).wait()
    sent = recv.at[:, :, pl.ds(0, FRAMES - OWN)]
    pltpu.make_async_copy(sent, sent, send_sem).wait()
    sent = obuf.at[:, :, pl.ds(0, FRAMES - OWN)]
    pltpu.make_async_copy(sent, sent, osend_sem).wait()


def body(queries, key_rows, values, cotangent, lengths, episode_cuts, gain_q, gain_k):
    smem = pl.BlockSpec(memory_space=pltpu.SMEM)
    vmem = pl.BlockSpec(memory_space=pltpu.VMEM)
    hbm = pl.BlockSpec(memory_space=pl.ANY)
    dma = pltpu.SemaphoreType.DMA
    width = HEADS * HD
    out, gain = pl.pallas_call(
        kernel,
        out_shape=(
            jax.ShapeDtypeStruct((3, OWN, PATCHES, width), BF16),
            jax.ShapeDtypeStruct((2, HD), F32),
        ),
        in_specs=[smem, smem, vmem, vmem, hbm, hbm, hbm, hbm],
        out_specs=(hbm, vmem),
        scratch_shapes=[
            pltpu.VMEM((4, OWN, PATCHES, width), BF16),
            pltpu.VMEM((GH, 4, FRAMES, TILE, HD), BF16),
            pltpu.VMEM((GH, 3, FRAMES, TILE, HD), BF16),
            pltpu.VMEM((ROWS, HD), BF16),
            pltpu.VMEM((ROWS, HD), BF16),
            pltpu.VMEM((ROWS, ROWS), BF16),
            pltpu.VMEM((ROWS, ROWS), BF16),
            pltpu.VMEM((ROWS, ROWS), F32),
            pltpu.VMEM((2, 8, HD), F32),
            pltpu.VMEM((2, 8, HD), F32),
            pltpu.VMEM((2, HD), F32),
            pltpu.VMEM((ZS, 2, HD), F32),
            pltpu.VMEM((ZS, 2, HD), F32),
            pltpu.VMEM((ZS, 2, HD), F32),
            pltpu.VMEM((2, HD), F32),
            pltpu.VMEM((SEQ, 2, HD), F32),
            dma, dma, dma((GH,)), dma, dma,
            dma, dma, dma, dma, dma, dma,
        ],
        compiler_params=pltpu.CompilerParams(
            collective_id=0, has_side_effects=True, vmem_limit_bytes=40 * 2**20
        ),
    )(
        lengths, episode_cuts, gain_q.reshape(1, SLICE), gain_k.reshape(1, SLICE),
        *(a.reshape(OWN, PATCHES, width) for a in (queries, key_rows, values, cotangent)),
    )
    return (out[0][None], out[1][None], out[2][None], gain[0, :SLICE], gain[1, :SLICE])


def solution(mesh):
    rows = P("clip", "seq", None, None)
    return jax.shard_map(
        body,
        mesh=mesh,
        in_specs=(rows, rows, rows, rows, P("clip"), P("clip", None), P("clip"), P("clip")),
        out_specs=(rows, rows, rows, P("clip"), P("clip")),
        check_vma=False,
    )
```

time: 475 us -> 138 us (0.29)
  blocking collectives: 281 us -> 0 us
  Pallas kernels: 0 us -> 129 us
  waiting for transfers between devices: 71.7 us -> 0 us
  starting transfers between devices: 61.6 us -> 0 us
  local copies, waits for them, and re-layouts: 37.6 us -> 8.13 us
  matrix products: 9.48 us -> 0 us
  other arithmetic: 9.11 us -> 0 us
    unnamed x2 -> x0, blocking collectives: 231 us -> none
    pallas_call x0 -> x1, Pallas kernels: none -> 129 us  [body(): pl.pallas_call(kernel, out_shape=(jax.ShapeDtypeStruct((3, OWN, PATCHES,...]
    all_to_all x7 -> x0, waiting for transfers between devices: 71.7 us -> none  [the longest x1 18.5 us: body(): lax.all_to_all(key_rows, 'seq', split_axis=2, concat_axis=1, tiled=True)]
    all_to_all x7 -> x0, starting transfers between devices: 61.6 us -> none  [the longest x1 33 us: body(): lax.all_to_all(values, 'seq', split_axis=2, concat_axis=1, tiled=True)]
    psum x1 -> x0, blocking collectives: 50.4 us -> none  [body(): seq_q, seq_k = lax.psum((part_q, part_k), 'seq')]
    convert_element_type x11 -> x0, local copies, waits for them, and re-layouts: 14.9 us -> none  [the longest x6 9.41 us: normalize(): values_f = split_heads(raw_rows.astype(jnp.float32), head_count)]
    dot_general x6 -> x0, matrix products: 9.48 us -> none  [the longest x1 2.81 us: attend(): jnp.einsum('bchts,bschd->btchd', ds_round, k_heads, preferred_element_typ...]
    unnamed x46 -> x14, local copies, waits for them, and re-layouts: 12.6 us -> 6.31 us
  transfers between devices with their start and end apart: 7 -> 0, of which waited for: 5 -> 0; matrix products, arithmetic and copies ran while one was open for 7% -> 0% of each run, Pallas kernels for 0% -> 0%
where the time goes in v1:
time: 138 us
  Pallas kernels  129 us (93%)
  local copies, waits for them, and re-layouts  8.13 us (6%)
    pallas_call x1, Pallas kernels, body(): pl.pallas_call(kernel, out_shape=(jax.ShapeDtypeStruct((3, OWN, PATCHES,...  129 us
    unnamed x14, local copies, waits for them, and re-layouts  6.31 us

profile of v1, /device:TPU:1, one launch (start us, length us, event | category | flops | bytes accessed | tf_op | source)
XLA Modules:
  0.0 138.1 jit_solution(10239306515975049034)
XLA Ops:
  1.3 0.0 copy-start
  1.3 1.1 copy-done
  2.4 0.0 copy-start.1
  2.4 1.1 copy-done.1
  3.5 0.0 copy-start.2
  3.5 1.1 copy-done.2
  4.5 0.0 copy-start.3
  4.5 1.1 copy-done.3
  5.6 0.0 copy-start.4
  5.6 0.7 copy-done.4
  6.3 0.0 copy-start.5
  6.3 0.7 copy-done.5
  6.9 0.0 copy-start.6
  6.9 0.7 copy-done.6
  7.6 128.6 %shard_map.119 = (bf16[3,2,64,2560]{3,2,1,0:T(8,128)(2,1)S(1)}, f32[2,128]{1,0:T(2,128)S(1)}) custom-call(s32[1]{0:T(128)S(6)} %copy.13.len_ref, s32[1,2]{1,0:T(1,128)S(1)} %copy-done.4, f32[1,80]{1,0:T(1,128)S(1)} %bitcast.14, f32[1,80]{1,0:T(1,128)S(1)} %bitcast.15, bf16[2,64,2560]{2,1,0:T(8,128)(2,1)S(1)} %bitcast.10, bf16[2,64,2560]{2,1,0:T(8,128)(2,1)S(1)} %bitcast.11, ...), custom_call_target="tpu_custom_call" | custom-call | tf_op jit(solution)/shard_map/pallas_call | solution.py:270
  136.2 1.3 fusion
  137.5 0.5 slice_bitcast_fusion
Async XLA Ops:
  1.3 1.1 copy-start
  2.4 1.1 copy-start.1
  3.5 1.1 copy-start.2
  4.5 1.1 copy-start.3
  5.6 0.7 copy-start.4
  6.3 0.7 copy-start.5
  6.9 0.7 copy-start.6

commit v2 on v1

--- a/solution.py
+++ b/solution.py
@@ -43,75 +43,77 @@
     return jnp.where(lane < HD - off, low, high)
 
 
+PEERS = [(dy, dc) for dy in (4, 3, -3, 2, -2, 1, -1) for dc in (0, 1)] + [(0, 1)]
+EARLY = 2
+
+
 def kernel(
-    len_ref, cut_ref, gq_ref, gk_ref, q_hbm, k_hbm, v_hbm, g_hbm,
-    o_hbm, gain_out,
+    len_hbm, cut_hbm, gq_hbm, gk_hbm, q_hbm, k_hbm, v_hbm, g_hbm,
+    o_ref, gain_out,
+    len_ref, cut_ref, gq_ref, gk_ref,
     stage, recv, obuf, qh_s, kh_s, soft_s, ds_s, bias, gains, parts,
-    gsend, grecv, psend, precv, fsend, frecv,
-    stage_sem, send_sem, recv_sem, osend_sem, orecv_sem,
-    gsend_sem, grecv_sem, psend_sem, precv_sem, fsend_sem, frecv_sem,
+    gsend, gmid, grecv, psend, precv, asend, brecv, csend, crecv,
+    small_sem, stage_sem, send_sem, recv_sem, osend_sem, orecv_sem,
+    gsend_sem, gmid_sem, hsend_sem, grecv_sem,
+    asend_sem, arecv_sem, bsend_sem, brecv_sem, csend_sem, crecv_sem,
 ):
     clip = lax.axis_index("clip")
     me = lax.axis_index("seq")
     x, z = lax.div(clip, ZS), lax.rem(clip, ZS)
     g, j = lax.div(me, TILES), lax.rem(me, TILES)
-    far_seq = x * TILES + j
-    same = (g == x).astype(jnp.int32)
-
-    def far(zz):
-        return (g * ZS + zz, far_seq)
-
-    def is_me(zz):
-        return jnp.logical_and(g == x, z == zz)
-
+    y, core = lax.div(me, 2), lax.rem(me, 2)
+    home = g == x
+
+    def seq_peer(n):
+        dy, dc = PEERS[n]
+        return lax.rem(y + (dy + 8), 8) * 2 + lax.rem(core + dc, 2)
+
+    def at_x(xx):
+        return (xx * ZS + z, me)
+
+    def at_z(zz):
+        return (x * ZS + zz, me)
+
+    def remote(src, dst, s_sem, r_sem, to):
+        pltpu.make_async_remote_copy(
+            src_ref=src, dst_ref=dst, send_sem=s_sem, recv_sem=r_sem,
+            device_id=to, device_id_type=MESH,
+        ).start()
+
+    def done(ref, sem):
+        pltpu.make_async_copy(ref, ref, sem).wait()
+
+    small = [
+        pltpu.make_async_copy(a, b, small_sem.at[n])
+        for n, (a, b) in enumerate(
+            ((gq_hbm, gq_ref), (gk_hbm, gk_ref), (len_hbm, len_ref), (cut_hbm, cut_ref))
+        )
+    ]
+    barrier = pltpu.get_barrier_semaphore()
+    others = [(clip, seq_peer(n)) for n in range(SEQ - 1)]
+    others += [at_x(lax.rem(x + d, XS)) for d in range(1, XS)]
+    others += [at_z(lax.rem(z + d, ZS)) for d in range(1, ZS)]
+    for to in others:
+        pl.semaphore_signal(barrier, inc=1, device_id=to, device_id_type=MESH)
     for n, ref in enumerate((q_hbm, k_hbm, v_hbm, g_hbm)):
         pltpu.make_async_copy(ref, stage.at[n], stage_sem).start()
-
-    barrier = pltpu.get_barrier_semaphore()
-    for d in range(1, SEQ):
-        pl.semaphore_signal(
-            barrier, inc=1, device_id=(clip, lax.rem(me + d, SEQ)), device_id_type=MESH
-        )
-    for zz in range(ZS):
-
-        @pl.when(jnp.logical_not(is_me(zz)))
-        def _():
-            pl.semaphore_signal(barrier, inc=1, device_id=far(zz), device_id_type=MESH)
+    for copy in small:
+        copy.start()
+    for copy in small:
+        copy.wait()
 
     gsend[...] = jnp.zeros_like(gsend)
     gsend[0:1, 0:SLICE] = gq_ref[...]
     gsend[1:2, 0:SLICE] = gk_ref[...]
-
-    def exchange(src, dst, s_sem, r_sem):
-        for zz in range(ZS):
-
-            @pl.when(is_me(zz))
-            def _():
-                pltpu.make_async_copy(src(zz), dst.at[z], r_sem).start()
-
-            @pl.when(jnp.logical_not(is_me(zz)))
-            def _():
-                pltpu.make_async_remote_copy(
-                    src_ref=src(zz), dst_ref=dst.at[z], send_sem=s_sem, recv_sem=r_sem,
-                    device_id=far(zz), device_id_type=MESH,
-                ).start()
-
-    def exchange_sent(dst, s_sem):
-        @pl.when(same == 1)
-        def _():
-            part = dst.at[pl.ds(0, ZS - 1)]
-            pltpu.make_async_copy(part, part, s_sem).wait()
-
-        @pl.when(same == 0)
-        def _():
-            pltpu.make_async_copy(dst, dst, s_sem).wait()
-
-    pltpu.make_async_copy(stage, stage, stage_sem).wait()
-    pl.semaphore_wait(barrier, SEQ - 1 + ZS - same)
-
-    exchange(lambda zz: gsend, grecv, gsend_sem, grecv_sem)
-
-    def send_in(h, _):
+    done(stage, stage_sem)
+    pl.semaphore_wait(barrier, len(others))
+
+    @pl.when(home)
+    def _():
+        for d in range(1, XS):
+            remote(gsend, gmid, gsend_sem, gmid_sem, at_x(lax.rem(x + d, XS)))
+
+    def send_in(h):
         def source(to):
             to_g, to_j = lax.div(to, TILES), lax.rem(to, TILES)
             return stage.at[
@@ -120,16 +122,33 @@
             ]
 
         place = recv.at[h, :, pl.ds(me * OWN, OWN)]
-        for d in range(1, SEQ):
-            to = lax.rem(me + d, SEQ)
-            pltpu.make_async_remote_copy(
-                src_ref=source(to), dst_ref=place, send_sem=send_sem, recv_sem=recv_sem.at[h],
-                device_id=(clip, to), device_id_type=MESH,
-            ).start()
+        for n in range(SEQ - 1):
+            to = seq_peer(n)
+            remote(source(to), place, send_sem, recv_sem.at[h], (clip, to))
         pltpu.make_async_copy(source(me), place, recv_sem.at[h]).start()
-        return 0
-
-    lax.fori_loop(0, GH, send_in, 0)
+
+    def loop(lo, hi, step):
+        def run(h, _):
+            step(h)
+            return 0
+
+        lax.fori_loop(lo, hi, run, 0)
+
+    loop(0, 2, send_in)
+
+    @pl.when(home)
+    def _():
+        gmid[...] = gsend[...]
+
+    @pl.when(jnp.logical_not(home))
+    def _():
+        done(gmid, gmid_sem)
+
+    for d in range(1, ZS):
+        remote(gmid, grecv.at[z], hsend_sem, grecv_sem, at_z(lax.rem(z + d, ZS)))
+    pltpu.make_async_copy(gmid, grecv.at[z], grecv_sem).start()
+
+    loop(2, GH, send_in)
 
     length = len_ref[0]
     cut_a, cut_b = cut_ref[0, 0], cut_ref[0, 1]
@@ -143,7 +162,7 @@
         ok = (s_f <= t_f) & (s_e == t_e) & (t_f < length) & (s_at % TILE == t_at % TILE)
         bias[0:rows, tb * BLK : (tb + 1) * BLK] = jnp.where(ok, 0.0, -1e30)
 
-    pltpu.make_async_copy(grecv, grecv, grecv_sem).wait()
+    done(grecv, grecv_sem)
     gains[...] = jnp.zeros_like(gains)
     for zz in range(ZS):
         row, off = divmod(zz * SLICE, HD)
@@ -176,8 +195,8 @@
         obuf[h, n, lo // TILE : (lo + BLK) // TILE] = out.astype(BF16).reshape(BF, TILE, HD)
         return jnp.sum(normed * grad, axis=0, keepdims=True)
 
-    def head(h, _):
-        pltpu.make_async_copy(recv.at[h], recv.at[h], recv_sem.at[h]).wait()
+    def head(h):
+        done(recv.at[h], recv_sem.at[h])
         q_r, k_r, v_r, g_r = (recv.at[h, n] for n in range(4))
         gain_q = gains[0, pl.ds(h, 1), :]
         gain_k = gains[1, pl.ds(h, 1), :]
@@ -219,63 +238,92 @@
         parts[0, pl.ds(h, 1), :] = part_q
         parts[1, pl.ds(h, 1), :] = part_k
 
-        place = o_hbm.at[
+        @pl.when(h < EARLY)
+        def _():
+            send_out(h)
+
+    def send_out(h):
+        place = o_ref.at[
             :, :, pl.ds(pl.multiple_of(j * TILE, TILE), TILE),
             pl.ds(pl.multiple_of((g * GH + h) * HD, HD), HD),
         ]
-        for d in range(1, SEQ):
-            to = lax.rem(me + d, SEQ)
-            pltpu.make_async_remote_copy(
-                src_ref=obuf.at[h, :, pl.ds(to * OWN, OWN)], dst_ref=place,
-                send_sem=osend_sem, recv_sem=orecv_sem,
-                device_id=(clip, to), device_id_type=MESH,
-            ).start()
+        for n in range(SEQ - 1):
+            to = seq_peer(n)
+            remote(
+                obuf.at[h, :, pl.ds(to * OWN, OWN)], place, osend_sem, orecv_sem, (clip, to)
+            )
         pltpu.make_async_copy(obuf.at[h, :, pl.ds(me * OWN, OWN)], place, orecv_sem).start()
-        return 0
-
-    lax.fori_loop(0, GH, head, 0)
+
+    loop(0, GH, head)
 
     for zz in range(ZS):
         for n in range(2):
             psend[zz, n : n + 1, :] = lanes(lambda r: parts[n, r : r + 1, :], zz * SLICE)
-    exchange(lambda zz: psend.at[zz], precv, psend_sem, precv_sem)
-    pltpu.make_async_copy(precv, precv, precv_sem).wait()
-    fsend[...] = jnp.sum(precv[...], axis=0)
-    for d in range(1, SEQ):
-        pltpu.make_async_remote_copy(
-            src_ref=fsend, dst_ref=frecv.at[me], send_sem=fsend_sem, recv_sem=frecv_sem,
-            device_id=(clip, lax.rem(me + d, SEQ)), device_id_type=MESH,
-        ).start()
-    pltpu.make_async_copy(fsend, frecv.at[me], frecv_sem).start()
-    pltpu.make_async_copy(frecv, frecv, frecv_sem).wait()
-    gain_out[...] = jnp.sum(frecv[...], axis=0)
-
-    pltpu.make_async_copy(o_hbm, o_hbm, orecv_sem).wait()
-    exchange_sent(grecv, gsend_sem)
-    exchange_sent(precv, psend_sem)
-    sent = frecv.at[pl.ds(0, SEQ - 1)]
-    pltpu.make_async_copy(sent, sent, fsend_sem).wait()
-    sent = recv.at[:, :, pl.ds(0, FRAMES - OWN)]
-    pltpu.make_async_copy(sent, sent, send_sem).wait()
-    sent = obuf.at[:, :, pl.ds(0, FRAMES - OWN)]
-    pltpu.make_async_copy(sent, sent, osend_sem).wait()
+    for d in range(1, ZS):
+        zz = lax.rem(z + d, ZS)
+        remote(psend.at[zz], precv.at[z], asend_sem, arecv_sem, at_z(zz))
+    pltpu.make_async_copy(psend.at[z], precv.at[z], arecv_sem).start()
+    send_out(EARLY)
+    done(precv, arecv_sem)
+    asend[...] = jnp.sum(precv[...], axis=0)
+
+    @pl.when(home)
+    def _():
+        pltpu.make_async_copy(asend, brecv.at[x], brecv_sem).start()
+
+    @pl.when(jnp.logical_not(home))
+    def _():
+        remote(asend, brecv.at[x], bsend_sem, brecv_sem, at_x(g))
+
+    send_out(EARLY + 1)
+
+    @pl.when(home)
+    def _():
+        done(brecv, brecv_sem)
+        csend[...] = jnp.sum(brecv[...], axis=0)
+        for n in range(SEQ - 1):
+            remote(csend, crecv.at[j], csend_sem, crecv_sem, (clip, seq_peer(n)))
+        pltpu.make_async_copy(csend, crecv.at[j], crecv_sem).start()
+
+    send_out(EARLY + 2)
+    done(crecv.at[pl.ds(0, TILES)], crecv_sem)
+    gain_out[...] = jnp.sum(crecv[0:TILES], axis=0)
+
+    @pl.when(home)
+    def _():
+        done(brecv.at[pl.ds(0, XS - 1)], gsend_sem)
+        done(crecv.at[pl.ds(0, SEQ - 1)], csend_sem)
+
+    @pl.when(jnp.logical_not(home))
+    def _():
+        done(asend, bsend_sem)
+
+    done(grecv.at[pl.ds(0, ZS - 1)], hsend_sem)
+    done(precv.at[pl.ds(0, ZS - 1)], asend_sem)
+    done(recv.at[:, :, pl.ds(0, FRAMES - OWN)], send_sem)
+    done(obuf.at[:, :, pl.ds(0, FRAMES - OWN)], osend_sem)
+    done(o_ref, orecv_sem)
 
 
 def body(queries, key_rows, values, cotangent, lengths, episode_cuts, gain_q, gain_k):
-    smem = pl.BlockSpec(memory_space=pltpu.SMEM)
     vmem = pl.BlockSpec(memory_space=pltpu.VMEM)
-    hbm = pl.BlockSpec(memory_space=pl.ANY)
+    hbm = pl.BlockSpec(memory_space=pltpu.HBM)
     dma = pltpu.SemaphoreType.DMA
     width = HEADS * HD
+    row = pltpu.VMEM((2, HD), F32)
     out, gain = pl.pallas_call(
         kernel,
         out_shape=(
             jax.ShapeDtypeStruct((3, OWN, PATCHES, width), BF16),
             jax.ShapeDtypeStruct((2, HD), F32),
         ),
-        in_specs=[smem, smem, vmem, vmem, hbm, hbm, hbm, hbm],
+        in_specs=[hbm] * 8,
         out_specs=(hbm, vmem),
         scratch_shapes=[
+            pltpu.SMEM((1,), jnp.int32),
+            pltpu.SMEM((1, 2), jnp.int32),
+            pltpu.VMEM((1, SLICE), F32),
+            pltpu.VMEM((1, SLICE), F32),
             pltpu.VMEM((4, OWN, PATCHES, width), BF16),
             pltpu.VMEM((GH, 4, FRAMES, TILE, HD), BF16),
             pltpu.VMEM((GH, 3, FRAMES, TILE, HD), BF16),
@@ -286,17 +334,21 @@
             pltpu.VMEM((ROWS, ROWS), F32),
             pltpu.VMEM((2, 8, HD), F32),
             pltpu.VMEM((2, 8, HD), F32),
-            pltpu.VMEM((2, HD), F32),
+            row,
+            row,
             pltpu.VMEM((ZS, 2, HD), F32),
             pltpu.VMEM((ZS, 2, HD), F32),
             pltpu.VMEM((ZS, 2, HD), F32),
-            pltpu.VMEM((2, HD), F32),
+            row,
+            pltpu.VMEM((XS, 2, HD), F32),
+            row,
             pltpu.VMEM((SEQ, 2, HD), F32),
-            dma, dma, dma((GH,)), dma, dma,
+            dma((4,)), dma, dma, dma((GH,)), dma, dma,
+            dma, dma, dma, dma,
             dma, dma, dma, dma, dma, dma,
         ],
         compiler_params=pltpu.CompilerParams(
-            collective_id=0, has_side_effects=True, vmem_limit_bytes=40 * 2**20
+            collective_id=0, has_side_effects=True, vmem_limit_bytes=60 * 2**20
         ),
     )(
         lengths, episode_cuts, gain_q.reshape(1, SLICE), gain_k.reshape(1, SLICE),

time: 138 us -> 119 us (0.86)
  Pallas kernels: 129 us -> 114 us
  local copies, waits for them, and re-layouts: 8.13 us -> 3.32 us
    pallas_call x1, Pallas kernels: 129 us -> 114 us  [body(): pl.pallas_call(kernel, out_shape=(jax.ShapeDtypeStruct((3, OWN, PATCHES,...]
    unnamed x14 -> x2, local copies, waits for them, and re-layouts: 6.31 us -> 0.01 us
    slice x1, local copies, waits for them, and re-layouts: 1.31 us -> 2.79 us  [body(): out[2][None]]
where the time goes in v2:
time: 119 us; the launch traced here: 118 us
  Pallas kernels  114 us (96%)
  local copies, waits for them, and re-layouts  3.32 us (3%)
  between operations  1.3 us (1%)
    pallas_call x1, Pallas kernels, body(): pl.pallas_call(kernel, out_shape=(jax.ShapeDtypeStruct((3, OWN, PATCHES,...  114 us
    slice x1, local copies, waits for them, and re-layouts, body(): out[2][None]  2.79 us

profile of v2, /device:TPU:1, one launch (start us, length us, event | category | flops | bytes accessed | tf_op | source)
XLA Modules:
  0.0 118.5 jit_solution(14105794595730330089)
XLA Ops:
  1.3 113.8 %shard_map.119 = (bf16[3,2,64,2560]{3,2,1,0:T(8,128)(2,1)}, f32[2,128]{1,0:T(2,128)}) custom-call(s32[1]{0:T(128)S(6)} %copy.13.len_hbm, s32[1,2]{1,0:T(1,128)} %cut_hbm.1, f32[1,80]{1,0:T(1,128)} %bitcast.14, f32[1,80]{1,0:T(1,128)} %bitcast.15, bf16[2,64,2560]{2,1,0:T(8,128)(2,1)} %bitcast.10, bf16[2,64,2560]{2,1,0:T(8,128)(2,1)} %bitcast.11, ...), custom_call_target="tpu_custom_call" | custom-call | tf_op jit(solution)/shard_map/pallas_call | solution.py:314
  115.1 0.0 copy-start
  115.1 2.8 %fusion = (bf16[1,2,64,2560]{3,2,1,0:T(8,128)(2,1)}, bf16[1,2,64,2560]{3,2,1,0:T(8,128)(2,1)}, bf16[1,2,64,2560]{3,2,1,0:T(8,128)(2,1)}) fusion(bf16[3,2,64,2560]{3,2,1,0:T(8,128)(2,1)} %get-tuple-element.7), kind=kLoop, calls=%fused_computation.2 | loop fusion | bytes 3932160 | tf_op jit(solution)/shard_map/slice | solution.py:357
  117.9 0.0 copy-done
  117.9 0.5 slice_bitcast_fusion
Async XLA Ops:
  115.1 2.8 %copy-start = (f32[2,128]{1,0:T(2,128)S(1)}, f32[2,128]{1,0:T(2,128)}, u32[]{:S(2)}) copy-start(f32[2,128]{1,0:T(2,128)} %get-tuple-element.8) | copy-start | bytes 3076

commit v3 on v2

--- a/solution.py
+++ b/solution.py
@@ -48,9 +48,9 @@
 
 
 def kernel(
-    len_hbm, cut_hbm, gq_hbm, gk_hbm, q_hbm, k_hbm, v_hbm, g_hbm,
+    len_ref, cut_hbm, gq_hbm, gk_hbm, q_hbm, k_hbm, v_hbm, g_hbm,
     o_ref, gain_out,
-    len_ref, cut_ref, gq_ref, gk_ref,
+    cut_ref, gq_ref, gk_ref,
     stage, recv, obuf, qh_s, kh_s, soft_s, ds_s, bias, gains, parts,
     gsend, gmid, grecv, psend, precv, asend, brecv, csend, crecv,
     small_sem, stage_sem, send_sem, recv_sem, osend_sem, orecv_sem,
@@ -86,7 +86,7 @@
     small = [
         pltpu.make_async_copy(a, b, small_sem.at[n])
         for n, (a, b) in enumerate(
-            ((gq_hbm, gq_ref), (gk_hbm, gk_ref), (len_hbm, len_ref), (cut_hbm, cut_ref))
+            ((gq_hbm, gq_ref), (gk_hbm, gk_ref), (cut_hbm, cut_ref))
         )
     ]
     barrier = pltpu.get_barrier_semaphore()
@@ -314,13 +314,12 @@
     out, gain = pl.pallas_call(
         kernel,
         out_shape=(
-            jax.ShapeDtypeStruct((3, OWN, PATCHES, width), BF16),
-            jax.ShapeDtypeStruct((2, HD), F32),
+            pltpu.VMEM((3, OWN, PATCHES, width), BF16),
+            pltpu.VMEM((2, HD), F32),
         ),
-        in_specs=[hbm] * 8,
-        out_specs=(hbm, vmem),
+        in_specs=[pl.BlockSpec(memory_space=pltpu.SMEM)] + [hbm] * 7,
+        out_specs=(vmem, vmem),
         scratch_shapes=[
-            pltpu.SMEM((1,), jnp.int32),
             pltpu.SMEM((1, 2), jnp.int32),
             pltpu.VMEM((1, SLICE), F32),
             pltpu.VMEM((1, SLICE), F32),
@@ -343,16 +342,22 @@
             pltpu.VMEM((XS, 2, HD), F32),
             row,
             pltpu.VMEM((SEQ, 2, HD), F32),
-            dma((4,)), dma, dma, dma((GH,)), dma, dma,
+            dma((3,)), dma, dma, dma((GH,)), dma, dma,
             dma, dma, dma, dma,
             dma, dma, dma, dma, dma, dma,
         ],
         compiler_params=pltpu.CompilerParams(
-            collective_id=0, has_side_effects=True, vmem_limit_bytes=60 * 2**20
+            collective_id=0, has_side_effects=True, vmem_limit_bytes=40 * 2**20
         ),
     )(
-        lengths, episode_cuts, gain_q.reshape(1, SLICE), gain_k.reshape(1, SLICE),
-        *(a.reshape(OWN, PATCHES, width) for a in (queries, key_rows, values, cotangent)),
+        lengths,
+        *(
+            pltpu.with_memory_space_constraint(a, pltpu.HBM)
+            for a in (
+                episode_cuts, gain_q.reshape(1, SLICE), gain_k.reshape(1, SLICE),
+                *(a.reshape(OWN, PATCHES, width) for a in (queries, key_rows, values, cotangent)),
+            )
+        )
     )
     return (out[0][None], out[1][None], out[2][None], gain[0, :SLICE], gain[1, :SLICE])
 

time: 119 us -> 116 us (0.975)
  local copies, waits for them, and re-layouts: 3.32 us -> 1.83 us
    slice x1, local copies, waits for them, and re-layouts: 2.79 us -> 1.31 us  [body(): out[2][None]]
where the time goes in v3:
time: 116 us
  Pallas kernels  113 us (97%)
  local copies, waits for them, and re-layouts  1.83 us (2%)
  between operations  1.29 us (1%)
    pallas_call x1, Pallas kernels, body(): pl.pallas_call(kernel, out_shape=(pltpu.VMEM((3, OWN, PATCHES, width), BF...  113 us

profile of v3, /device:TPU:1, one launch (start us, length us, event | category | flops | bytes accessed | tf_op | source)
XLA Modules:
  0.0 116.3 jit_solution(8304587460971457188)
XLA Ops:
  1.3 113.2 %shard_map.119 = (bf16[3,2,64,2560]{3,2,1,0:T(8,128)(2,1)S(1)}, f32[2,128]{1,0:T(2,128)S(1)}) custom-call(s32[1]{0:T(128)S(6)} %copy.13.len_ref, s32[1,2]{1,0:T(1,128)} %cut_hbm.1, f32[1,80]{1,0:T(1,128)} %bitcast.14, f32[1,80]{1,0:T(1,128)} %bitcast.15, bf16[2,64,2560]{2,1,0:T(8,128)(2,1)} %bitcast.10, bf16[2,64,2560]{2,1,0:T(8,128)(2,1)} %bitcast.11, ...), custom_call_target="tpu_custom_call" | custom-call | tf_op jit(solution)/shard_map/pallas_call | solution.py:314
  114.4 1.3 %fusion = (bf16[1,2,64,2560]{3,2,1,0:T(8,128)(2,1)}, bf16[1,2,64,2560]{3,2,1,0:T(8,128)(2,1)}, bf16[1,2,64,2560]{3,2,1,0:T(8,128)(2,1)}) fusion(bf16[3,2,64,2560]{3,2,1,0:T(8,128)(2,1)S(1)} %get-tuple-element.7), kind=kLoop, calls=%fused_computation.2 | loop fusion | bytes 3932160 | tf_op jit(solution)/shard_map/slice | solution.py:362
  115.8 0.5 slice_bitcast_fusion

commit v4 on v3

--- a/solution.py
+++ b/solution.py
@@ -44,7 +44,7 @@
 
 
 PEERS = [(dy, dc) for dy in (4, 3, -3, 2, -2, 1, -1) for dc in (0, 1)] + [(0, 1)]
-EARLY = 2
+EARLY = 1
 
 
 def kernel(
@@ -52,9 +52,9 @@
     o_ref, gain_out,
     cut_ref, gq_ref, gk_ref,
     stage, recv, obuf, qh_s, kh_s, soft_s, ds_s, bias, gains, parts,
-    gsend, gmid, grecv, psend, precv, asend, brecv, csend, crecv,
+    gsend, gmid, grecv, parts_in, psend, precv, asend, brecv, csend, crecv, ready,
     small_sem, stage_sem, send_sem, recv_sem, osend_sem, orecv_sem,
-    gsend_sem, gmid_sem, hsend_sem, grecv_sem,
+    gsend_sem, gmid_sem, hsend_sem, grecv_sem, pass_sem, pair_sem,
     asend_sem, arecv_sem, bsend_sem, brecv_sem, csend_sem, crecv_sem,
 ):
     clip = lax.axis_index("clip")
@@ -62,7 +62,11 @@
     x, z = lax.div(clip, ZS), lax.rem(clip, ZS)
     g, j = lax.div(me, TILES), lax.rem(me, TILES)
     y, core = lax.div(me, 2), lax.rem(me, 2)
+    agent = core == 0
     home = g == x
+    inner = jnp.logical_and(agent, home)
+    outer = jnp.logical_and(agent, jnp.logical_not(home))
+    other = (clip, me + 1 - 2 * core)
 
     def seq_peer(n):
         dy, dc = PEERS[n]
@@ -90,11 +94,21 @@
         )
     ]
     barrier = pltpu.get_barrier_semaphore()
-    others = [(clip, seq_peer(n)) for n in range(SEQ - 1)]
-    others += [at_x(lax.rem(x + d, XS)) for d in range(1, XS)]
-    others += [at_z(lax.rem(z + d, ZS)) for d in range(1, ZS)]
-    for to in others:
+
+    def greet(to):
         pl.semaphore_signal(barrier, inc=1, device_id=to, device_id_type=MESH)
+
+    for dy in (4, 3, -3, 2, -2, 1, -1):
+        greet((clip, lax.rem(y + (dy + 8), 8) * 2 + 1))
+
+    @pl.when(agent)
+    def _():
+        greet(other)
+        for d in range(1, XS):
+            greet(at_x(lax.rem(x + d, XS)))
+        for d in range(1, ZS):
+            greet(at_z(lax.rem(z + d, ZS)))
+
     for n, ref in enumerate((q_hbm, k_hbm, v_hbm, g_hbm)):
         pltpu.make_async_copy(ref, stage.at[n], stage_sem).start()
     for copy in small:
@@ -105,13 +119,18 @@
     gsend[...] = jnp.zeros_like(gsend)
     gsend[0:1, 0:SLICE] = gq_ref[...]
     gsend[1:2, 0:SLICE] = gk_ref[...]
+    parts[...] = jnp.zeros_like(parts)
+
+    @pl.when(core == 1)
+    def _():
+        pl.semaphore_wait(barrier, SEQ - 1)
+        pl.semaphore_signal(ready, inc=1, device_id=other, device_id_type=MESH)
+
+    @pl.when(agent)
+    def _():
+        pl.semaphore_wait(ready, 1)
+
     done(stage, stage_sem)
-    pl.semaphore_wait(barrier, len(others))
-
-    @pl.when(home)
-    def _():
-        for d in range(1, XS):
-            remote(gsend, gmid, gsend_sem, gmid_sem, at_x(lax.rem(x + d, XS)))
 
     def send_in(h):
         def source(to):
@@ -134,21 +153,41 @@
 
         lax.fori_loop(lo, hi, run, 0)
 
-    loop(0, 2, send_in)
-
-    @pl.when(home)
+    loop(0, 1, send_in)
+
+    @pl.when(agent)
+    def _():
+        pl.semaphore_wait(barrier, XS - 1 + ZS - 1)
+
+    @pl.when(inner)
+    def _():
+        for d in range(1, XS):
+            remote(gsend, gmid, gsend_sem, gmid_sem, at_x(lax.rem(x + d, XS)))
+
+    loop(1, 2, send_in)
+
+    @pl.when(inner)
     def _():
         gmid[...] = gsend[...]
 
-    @pl.when(jnp.logical_not(home))
+    @pl.when(outer)
     def _():
         done(gmid, gmid_sem)
 
-    for d in range(1, ZS):
-        remote(gmid, grecv.at[z], hsend_sem, grecv_sem, at_z(lax.rem(z + d, ZS)))
-    pltpu.make_async_copy(gmid, grecv.at[z], grecv_sem).start()
-
-    loop(2, GH, send_in)
+    @pl.when(agent)
+    def _():
+        for d in range(1, ZS):
+            remote(gmid, grecv.at[z], hsend_sem, grecv_sem, at_z(lax.rem(z + d, ZS)))
+        pltpu.make_async_copy(gmid, grecv.at[z], grecv_sem).start()
+
+    loop(2, 3, send_in)
+
+    @pl.when(agent)
+    def _():
+        done(grecv, grecv_sem)
+        remote(grecv, grecv, pass_sem, grecv_sem, other)
+
+    loop(3, GH, send_in)
 
     length = len_ref[0]
     cut_a, cut_b = cut_ref[0, 0], cut_ref[0, 1]
@@ -162,7 +201,10 @@
         ok = (s_f <= t_f) & (s_e == t_e) & (t_f < length) & (s_at % TILE == t_at % TILE)
         bias[0:rows, tb * BLK : (tb + 1) * BLK] = jnp.where(ok, 0.0, -1e30)
 
-    done(grecv, grecv_sem)
+    @pl.when(core == 1)
+    def _():
+        done(grecv, grecv_sem)
+
     gains[...] = jnp.zeros_like(gains)
     for zz in range(ZS):
         row, off = divmod(zz * SLICE, HD)
@@ -256,50 +298,73 @@
 
     loop(0, GH, head)
 
-    for zz in range(ZS):
-        for n in range(2):
-            psend[zz, n : n + 1, :] = lanes(lambda r: parts[n, r : r + 1, :], zz * SLICE)
-    for d in range(1, ZS):
-        zz = lax.rem(z + d, ZS)
-        remote(psend.at[zz], precv.at[z], asend_sem, arecv_sem, at_z(zz))
-    pltpu.make_async_copy(psend.at[z], precv.at[z], arecv_sem).start()
+    @pl.when(core == 1)
+    def _():
+        remote(parts, parts_in, pass_sem, pair_sem, other)
+
     send_out(EARLY)
-    done(precv, arecv_sem)
-    asend[...] = jnp.sum(precv[...], axis=0)
-
-    @pl.when(home)
+
+    @pl.when(agent)
+    def _():
+        done(parts_in, pair_sem)
+        parts[...] += parts_in[...]
+        for zz in range(ZS):
+            for n in range(2):
+                psend[zz, n : n + 1, :] = lanes(lambda r: parts[n, r : r + 1, :], zz * SLICE)
+        for d in range(1, ZS):
+            zz = lax.rem(z + d, ZS)
+            remote(psend.at[zz], precv.at[z], asend_sem, arecv_sem, at_z(zz))
+        pltpu.make_async_copy(psend.at[z], precv.at[z], arecv_sem).start()
+
+    send_out(EARLY + 1)
+
+    @pl.when(agent)
+    def _():
+        done(precv, arecv_sem)
+        asend[...] = jnp.sum(precv[...], axis=0)
+
+    @pl.when(inner)
     def _():
         pltpu.make_async_copy(asend, brecv.at[x], brecv_sem).start()
 
-    @pl.when(jnp.logical_not(home))
+    @pl.when(outer)
     def _():
         remote(asend, brecv.at[x], bsend_sem, brecv_sem, at_x(g))
 
-    send_out(EARLY + 1)
-
-    @pl.when(home)
+    send_out(EARLY + 2)
+
+    @pl.when(inner)
     def _():
         done(brecv, brecv_sem)
         csend[...] = jnp.sum(brecv[...], axis=0)
+        slot = lax.div(j, 2)
         for n in range(SEQ - 1):
-            remote(csend, crecv.at[j], csend_sem, crecv_sem, (clip, seq_peer(n)))
-        pltpu.make_async_copy(csend, crecv.at[j], crecv_sem).start()
-
-    send_out(EARLY + 2)
-    done(crecv.at[pl.ds(0, TILES)], crecv_sem)
-    gain_out[...] = jnp.sum(crecv[0:TILES], axis=0)
-
-    @pl.when(home)
+            remote(csend, crecv.at[slot], csend_sem, crecv_sem, (clip, seq_peer(n)))
+        pltpu.make_async_copy(csend, crecv.at[slot], crecv_sem).start()
+
+    send_out(EARLY + 3)
+    done(crecv.at[pl.ds(0, 2)], crecv_sem)
+    gain_out[...] = crecv[0] + crecv[1]
+
+    @pl.when(inner)
     def _():
         done(brecv.at[pl.ds(0, XS - 1)], gsend_sem)
         done(crecv.at[pl.ds(0, SEQ - 1)], csend_sem)
 
-    @pl.when(jnp.logical_not(home))
+    @pl.when(outer)
     def _():
         done(asend, bsend_sem)
 
-    done(grecv.at[pl.ds(0, ZS - 1)], hsend_sem)
-    done(precv.at[pl.ds(0, ZS - 1)], asend_sem)
+    @pl.when(agent)
+    def _():
+        done(grecv.at[pl.ds(0, ZS - 1)], hsend_sem)
+        done(precv.at[pl.ds(0, ZS - 1)], asend_sem)
+        done(grecv, pass_sem)
+
+    @pl.when(core == 1)
+    def _():
+        done(parts_in, pass_sem)
+
     done(recv.at[:, :, pl.ds(0, FRAMES - OWN)], send_sem)
     done(obuf.at[:, :, pl.ds(0, FRAMES - OWN)], osend_sem)
     done(o_ref, orecv_sem)
@@ -336,14 +401,16 @@
             row,
             row,
             pltpu.VMEM((ZS, 2, HD), F32),
+            pltpu.VMEM((2, 8, HD), F32),
             pltpu.VMEM((ZS, 2, HD), F32),
             pltpu.VMEM((ZS, 2, HD), F32),
             row,
             pltpu.VMEM((XS, 2, HD), F32),
             row,
             pltpu.VMEM((SEQ, 2, HD), F32),
+            pltpu.SemaphoreType.REGULAR,
             dma((3,)), dma, dma, dma((GH,)), dma, dma,
-            dma, dma, dma, dma,
+            dma, dma, dma, dma, dma, dma,
             dma, dma, dma, dma, dma, dma,
         ],
         compiler_params=pltpu.CompilerParams(

time: 116 us -> 113 us (0.974)
  Pallas kernels: 113 us -> 110 us
    pallas_call x1, Pallas kernels: 113 us -> 110 us  [body(): pl.pallas_call(kernel, out_shape=(pltpu.VMEM((3, OWN, PATCHES, width), BF...]
where the time goes in v4:
time: 113 us
  Pallas kernels  110 us (97%)
  local copies, waits for them, and re-layouts  1.83 us (2%)
  between operations  1.29 us (1%)
    pallas_call x1, Pallas kernels, body(): pl.pallas_call(kernel, out_shape=(pltpu.VMEM((3, OWN, PATCHES, width), BF...  110 us

profile of v4, /device:TPU:1, one launch (start us, length us, event | category | flops | bytes accessed | tf_op | source)
XLA Modules:
  0.0 112.8 jit_solution(5028583989323441109)
XLA Ops:
  1.3 109.7 %shard_map.119 = (bf16[3,2,64,2560]{3,2,1,0:T(8,128)(2,1)S(1)}, f32[2,128]{1,0:T(2,128)S(1)}) custom-call(s32[1]{0:T(128)S(6)} %copy.13.len_ref, s32[1,2]{1,0:T(1,128)} %cut_hbm.1, f32[1,80]{1,0:T(1,128)} %bitcast.14, f32[1,80]{1,0:T(1,128)} %bitcast.15, bf16[2,64,2560]{2,1,0:T(8,128)(2,1)} %bitcast.10, bf16[2,64,2560]{2,1,0:T(8,128)(2,1)} %bitcast.11, ...), custom_call_target="tpu_custom_call" | custom-call | tf_op jit(solution)/shard_map/pallas_call | solution.py:379
  111.0 1.3 %fusion = (bf16[1,2,64,2560]{3,2,1,0:T(8,128)(2,1)}, bf16[1,2,64,2560]{3,2,1,0:T(8,128)(2,1)}, bf16[1,2,64,2560]{3,2,1,0:T(8,128)(2,1)}) fusion(bf16[3,2,64,2560]{3,2,1,0:T(8,128)(2,1)S(1)} %get-tuple-element.7), kind=kLoop, calls=%fused_computation.2 | loop fusion | bytes 3932160 | tf_op jit(solution)/shard_map/slice | solution.py:429
  112.3 0.5 slice_bitcast_fusion

commit v5 on v4

--- a/solution.py
+++ b/solution.py
@@ -44,6 +44,8 @@
 
 
 PEERS = [(dy, dc) for dy in (4, 3, -3, 2, -2, 1, -1) for dc in (0, 1)] + [(0, 1)]
+ALIKE = [n for n, (_, dc) in enumerate(PEERS) if dc == 0]
+UNLIKE = [n for n, (_, dc) in enumerate(PEERS) if dc == 1]
 EARLY = 1
 
 
@@ -62,11 +64,10 @@
     x, z = lax.div(clip, ZS), lax.rem(clip, ZS)
     g, j = lax.div(me, TILES), lax.rem(me, TILES)
     y, core = lax.div(me, 2), lax.rem(me, 2)
-    agent = core == 0
+    agent = j == 0
     home = g == x
     inner = jnp.logical_and(agent, home)
     outer = jnp.logical_and(agent, jnp.logical_not(home))
-    other = (clip, me + 1 - 2 * core)
 
     def seq_peer(n):
         dy, dc = PEERS[n]
@@ -98,12 +99,26 @@
     def greet(to):
         pl.semaphore_signal(barrier, inc=1, device_id=to, device_id_type=MESH)
 
-    for dy in (4, 3, -3, 2, -2, 1, -1):
-        greet((clip, lax.rem(y + (dy + 8), 8) * 2 + 1))
-
-    @pl.when(agent)
-    def _():
-        greet(other)
+    def tell(to):
+        pl.semaphore_signal(ready, inc=1, device_id=(clip, to), device_id_type=MESH)
+
+    @pl.when(core == 1)
+    def _():
+        for dy in (4, 3, -3, 2, -2, 1, -1):
+            greet((clip, lax.rem(y + (dy + 8), 8) * 2 + 1))
+
+    @pl.when(j == 3)
+    def _():
+        greet((clip, me - 1))
+
+    @pl.when(core == 0)
+    def _():
+        for dg in (2, 1, 3):
+            greet((clip, lax.rem(g + dg, GROUPS) * TILES + 2))
+
+    @pl.when(agent)
+    def _():
+        greet((clip, me + 2))
         for d in range(1, XS):
             greet(at_x(lax.rem(x + d, XS)))
         for d in range(1, ZS):
@@ -113,26 +128,8 @@
         pltpu.make_async_copy(ref, stage.at[n], stage_sem).start()
     for copy in small:
         copy.start()
-    for copy in small:
-        copy.wait()
-
-    gsend[...] = jnp.zeros_like(gsend)
-    gsend[0:1, 0:SLICE] = gq_ref[...]
-    gsend[1:2, 0:SLICE] = gk_ref[...]
-    parts[...] = jnp.zeros_like(parts)
-
-    @pl.when(core == 1)
-    def _():
-        pl.semaphore_wait(barrier, SEQ - 1)
-        pl.semaphore_signal(ready, inc=1, device_id=other, device_id_type=MESH)
-
-    @pl.when(agent)
-    def _():
-        pl.semaphore_wait(ready, 1)
-
-    done(stage, stage_sem)
-
-    def send_in(h):
+
+    def send_to(h, peers):
         def source(to):
             to_g, to_j = lax.div(to, TILES), lax.rem(to, TILES)
             return stage.at[
@@ -141,10 +138,21 @@
             ]
 
         place = recv.at[h, :, pl.ds(me * OWN, OWN)]
-        for n in range(SEQ - 1):
+        for n in peers:
             to = seq_peer(n)
             remote(source(to), place, send_sem, recv_sem.at[h], (clip, to))
-        pltpu.make_async_copy(source(me), place, recv_sem.at[h]).start()
+        return source(me), place
+
+    def send_in(h):
+        mine, place = send_to(h, range(SEQ - 1))
+        pltpu.make_async_copy(mine, place, recv_sem.at[h]).start()
+
+    def send_alike(h):
+        send_to(h, ALIKE)
+
+    def send_unlike(h):
+        mine, place = send_to(h, UNLIKE)
+        pltpu.make_async_copy(mine, place, recv_sem.at[h]).start()
 
     def loop(lo, hi, step):
         def run(h, _):
@@ -153,7 +161,36 @@
 
         lax.fori_loop(lo, hi, run, 0)
 
-    loop(0, 1, send_in)
+    @pl.when(j == 2)
+    def _():
+        pl.semaphore_wait(barrier, SEQ // 2)
+        tell(me + 1)
+
+    @pl.when(core == 1)
+    def _():
+        pl.semaphore_wait(barrier, SEQ // 2 - 1)
+        done(stage, stage_sem)
+        loop(0, 2, send_alike)
+
+    pl.semaphore_wait(ready, 1)
+
+    @pl.when(j == 3)
+    def _():
+        for d in (3, 2, 1):
+            tell(me - d)
+
+    @pl.when(core == 0)
+    def _():
+        done(stage, stage_sem)
+        loop(0, 1, send_alike)
+
+    loop(0, 1, send_unlike)
+    for copy in small:
+        copy.wait()
+    gsend[...] = jnp.zeros_like(gsend)
+    gsend[0:1, 0:SLICE] = gq_ref[...]
+    gsend[1:2, 0:SLICE] = gk_ref[...]
+    parts[...] = jnp.zeros_like(parts)
 
     @pl.when(agent)
     def _():
@@ -164,7 +201,11 @@
         for d in range(1, XS):
             remote(gsend, gmid, gsend_sem, gmid_sem, at_x(lax.rem(x + d, XS)))
 
-    loop(1, 2, send_in)
+    @pl.when(core == 0)
+    def _():
+        loop(1, 2, send_alike)
+
+    loop(1, 2, send_unlike)
 
     @pl.when(inner)
     def _():
@@ -185,7 +226,8 @@
     @pl.when(agent)
     def _():
         done(grecv, grecv_sem)
-        remote(grecv, grecv, pass_sem, grecv_sem, other)
+        for d in range(1, TILES):
+            remote(grecv, grecv, pass_sem, grecv_sem, (clip, me + d))
 
     loop(3, GH, send_in)
 
@@ -201,7 +243,7 @@
         ok = (s_f <= t_f) & (s_e == t_e) & (t_f < length) & (s_at % TILE == t_at % TILE)
         bias[0:rows, tb * BLK : (tb + 1) * BLK] = jnp.where(ok, 0.0, -1e30)
 
-    @pl.when(core == 1)
+    @pl.when(jnp.logical_not(agent))
     def _():
         done(grecv, grecv_sem)
 
@@ -298,16 +340,16 @@
 
     loop(0, GH, head)
 
-    @pl.when(core == 1)
-    def _():
-        remote(parts, parts_in, pass_sem, pair_sem, other)
+    @pl.when(jnp.logical_not(agent))
+    def _():
+        remote(parts, parts_in.at[j - 1], pass_sem, pair_sem, (clip, me - j))
 
     send_out(EARLY)
 
     @pl.when(agent)
     def _():
         done(parts_in, pair_sem)
-        parts[...] += parts_in[...]
+        parts[...] += jnp.sum(parts_in[...], axis=0)
         for zz in range(ZS):
             for n in range(2):
                 psend[zz, n : n + 1, :] = lanes(lambda r: parts[n, r : r + 1, :], zz * SLICE)
@@ -337,14 +379,13 @@
     def _():
         done(brecv, brecv_sem)
         csend[...] = jnp.sum(brecv[...], axis=0)
-        slot = lax.div(j, 2)
         for n in range(SEQ - 1):
-            remote(csend, crecv.at[slot], csend_sem, crecv_sem, (clip, seq_peer(n)))
-        pltpu.make_async_copy(csend, crecv.at[slot], crecv_sem).start()
+            remote(csend, crecv.at[0], csend_sem, crecv_sem, (clip, seq_peer(n)))
+        pltpu.make_async_copy(csend, crecv.at[0], crecv_sem).start()
 
     send_out(EARLY + 3)
-    done(crecv.at[pl.ds(0, 2)], crecv_sem)
-    gain_out[...] = crecv[0] + crecv[1]
+    done(crecv.at[0], crecv_sem)
+    gain_out[...] = crecv[0]
 
     @pl.when(inner)
     def _():
@@ -359,11 +400,11 @@
     def _():
         done(grecv.at[pl.ds(0, ZS - 1)], hsend_sem)
         done(precv.at[pl.ds(0, ZS - 1)], asend_sem)
-        done(grecv, pass_sem)
-
-    @pl.when(core == 1)
-    def _():
         done(parts_in, pass_sem)
+
+    @pl.when(jnp.logical_not(agent))
+    def _():
+        done(parts_in.at[0], pass_sem)
 
     done(recv.at[:, :, pl.ds(0, FRAMES - OWN)], send_sem)
     done(obuf.at[:, :, pl.ds(0, FRAMES - OWN)], osend_sem)
@@ -401,7 +442,7 @@
             row,
             row,
             pltpu.VMEM((ZS, 2, HD), F32),
-            pltpu.VMEM((2, 8, HD), F32),
+            pltpu.VMEM((TILES - 1, 2, 8, HD), F32),
             pltpu.VMEM((ZS, 2, HD), F32),
             pltpu.VMEM((ZS, 2, HD), F32),
             row,

time: 113 us -> 110 us (0.973)
  Pallas kernels: 110 us -> 107 us
    pallas_call x1, Pallas kernels: 110 us -> 107 us  [body(): pl.pallas_call(kernel, out_shape=(pltpu.VMEM((3, OWN, PATCHES, width), BF...]
where the time goes in v5:
time: 110 us
  Pallas kernels  107 us (97%)
  local copies, waits for them, and re-layouts  1.83 us (2%)
  between operations  1.29 us (1%)
    pallas_call x1, Pallas kernels, body(): pl.pallas_call(kernel, out_shape=(pltpu.VMEM((3, OWN, PATCHES, width), BF...  107 us

profile of v5, /device:TPU:1, one launch (start us, length us, event | category | flops | bytes accessed | tf_op | source)
XLA Modules:
  0.0 110.3 jit_solution(5396137196382366880)
XLA Ops:
  1.3 107.2 %shard_map.119 = (bf16[3,2,64,2560]{3,2,1,0:T(8,128)(2,1)S(1)}, f32[2,128]{1,0:T(2,128)S(1)}) custom-call(s32[1]{0:T(128)S(6)} %copy.13.len_ref, s32[1,2]{1,0:T(1,128)} %cut_hbm.1, f32[1,80]{1,0:T(1,128)} %bitcast.14, f32[1,80]{1,0:T(1,128)} %bitcast.15, bf16[2,64,2560]{2,1,0:T(8,128)(2,1)} %bitcast.10, bf16[2,64,2560]{2,1,0:T(8,128)(2,1)} %bitcast.11, ...), custom_call_target="tpu_custom_call" | custom-call | tf_op jit(solution)/shard_map/pallas_call | solution.py:420
  108.5 1.3 %fusion = (bf16[1,2,64,2560]{3,2,1,0:T(8,128)(2,1)}, bf16[1,2,64,2560]{3,2,1,0:T(8,128)(2,1)}, bf16[1,2,64,2560]{3,2,1,0:T(8,128)(2,1)}) fusion(bf16[3,2,64,2560]{3,2,1,0:T(8,128)(2,1)S(1)} %get-tuple-element.7), kind=kLoop, calls=%fused_computation.2 | loop fusion | bytes 3932160 | tf_op jit(solution)/shard_map/slice | solution.py:470
  109.8 0.5 slice_bitcast_fusion

commit v6 on v5

--- a/solution.py
+++ b/solution.py
@@ -66,12 +66,13 @@
     y, core = lax.div(me, 2), lax.rem(me, 2)
     agent = j == 0
     home = g == x
+    way = 1 - 2 * core
     inner = jnp.logical_and(agent, home)
     outer = jnp.logical_and(agent, jnp.logical_not(home))
 
     def seq_peer(n):
         dy, dc = PEERS[n]
-        return lax.rem(y + (dy + 8), 8) * 2 + lax.rem(core + dc, 2)
+        return lax.rem(y + 8 + dy * way, 8) * 2 + lax.rem(core + dc, 2)
 
     def at_x(xx):
         return (xx * ZS + z, me)
@@ -409,6 +410,18 @@
     done(recv.at[:, :, pl.ds(0, FRAMES - OWN)], send_sem)
     done(obuf.at[:, :, pl.ds(0, FRAMES - OWN)], osend_sem)
     done(o_ref, orecv_sem)
+
+
+def unpack(o_ref, gain, out_q, out_k, out_v, gain_q, gain_k, line_q, line_k, sems):
+    line_q[...] = gain[0:1, 0:SLICE]
+    line_k[...] = gain[1:2, 0:SLICE]
+    pairs = [(o_ref.at[n], ref) for n, ref in enumerate((out_q, out_k, out_v))]
+    pairs += [(line_q, gain_q), (line_k, gain_k)]
+    copies = [pltpu.make_async_copy(a, b, sems.at[n]) for n, (a, b) in enumerate(pairs)]
+    for copy in copies:
+        copy.start()
+    for copy in copies:
+        copy.wait()
 
 
 def body(queries, key_rows, values, cotangent, lengths, episode_cuts, gain_q, gain_k):
@@ -467,7 +480,16 @@
             )
         )
     )
-    return (out[0][None], out[1][None], out[2][None], gain[0, :SLICE], gain[1, :SLICE])
+    rows = pltpu.HBM((OWN, PATCHES, width), BF16)
+    line = pltpu.HBM((1, SLICE), F32)
+    *grads, grad_gq, grad_gk = pl.pallas_call(
+        unpack,
+        out_shape=(rows, rows, rows, line, line),
+        in_specs=[vmem, vmem],
+        out_specs=(hbm,) * 5,
+        scratch_shapes=[pltpu.VMEM((1, SLICE), F32), pltpu.VMEM((1, SLICE), F32), dma((5,))],
+    )(*(pltpu.with_memory_space_constraint(a, pltpu.VMEM) for a in (out, gain)))
+    return (*(a[None] for a in grads), grad_gq.reshape(SLICE), grad_gk.reshape(SLICE))
 
 
 def solution(mesh):

time: 110 us -> 110 us (level)
  Pallas kernels: 107 us -> 109 us
  local copies, waits for them, and re-layouts: 1.83 us -> 0 us
    pallas_call x0 -> x1, Pallas kernels: none -> 1.32 us  [body(): pl.pallas_call(unpack, out_shape=(rows, rows, rows, line, line), in_specs...]
    slice x1 -> x0, local copies, waits for them, and re-layouts: 1.31 us -> none  [body(): out[2][None]]
where the time goes in v6:
time: 110 us
  Pallas kernels  109 us (99%)
  between operations  1.29 us (1%)
    pallas_call x1, Pallas kernels, body(): pl.pallas_call(kernel, out_shape=(pltpu.VMEM((3, OWN, PATCHES, width), BF...  107 us

profile of v6, /device:TPU:1, one launch (start us, length us, event | category | flops | bytes accessed | tf_op | source)
XLA Modules:
  0.0 109.8 jit_solution(4811071799282672211)
XLA Ops:
  1.3 107.2 %shard_map.119 = (bf16[3,2,64,2560]{3,2,1,0:T(8,128)(2,1)S(1)}, f32[2,128]{1,0:T(2,128)S(1)}) custom-call(s32[1]{0:T(128)S(6)} %copy.13.len_ref, s32[1,2]{1,0:T(1,128)} %cut_hbm.1, f32[1,80]{1,0:T(1,128)} %bitcast.15, f32[1,80]{1,0:T(1,128)} %bitcast.16, bf16[2,64,2560]{2,1,0:T(8,128)(2,1)} %bitcast.11, bf16[2,64,2560]{2,1,0:T(8,128)(2,1)} %bitcast.12, ...), custom_call_target="tpu_custom_call" | custom-call | tf_op jit(solution)/shard_map/pallas_call | solution.py:433
  108.5 1.3 %shard_map.120 = (bf16[2,64,2560]{2,1,0:T(8,128)(2,1)}, bf16[2,64,2560]{2,1,0:T(8,128)(2,1)}, bf16[2,64,2560]{2,1,0:T(8,128)(2,1)}, f32[1,80]{1,0:T(1,128)}, f32[1,80]{1,0:T(1,128)}) custom-call(bf16[3,2,64,2560]{3,2,1,0:T(8,128)(2,1)S(1)} %get-tuple-element.12.o_ref, f32[2,128]{1,0:T(2,128)S(1)} %get-tuple-element.13.gain), custom_call_target="tpu_custom_call" | custom-call | tf_op jit(solution)/shard_map/pallas_call | solution.py:485
